TPU v7x, 32 devices: a whole 2x2x4 slice. The times are simulated.
32 devices in a mesh: seg: 8 (over y, x, core), stretch: 4 (over z).
Axes of the slice: x: 2, y: 2, z: 4, core: 2. Of those that a mesh axis runs over, the one named last changes fastest.
Arguments:
- queries: bfloat16 [1024, 8192], P('seg', 'stretch'), may hold values from -80 to 80
- branch_kv: bfloat16 [2, 1024, 1024], P(None, 'seg'), may hold values from -6 to 6
- prompt_kv: bfloat16 [2, 768, 1024], P(None, 'stretch'), may hold values from -4 to 4
- ancestry: int32 [8, 8], replicated, may hold values from 0 to 1, as said below
- segment_of_slot: int32 [8], replicated, may hold values from 0 to 7, each once
- counts: int32 [8], replicated, may hold values from 1 to 128, 768 in all
Outputs:
- attended: bfloat16 [1024, 8192], P('seg', 'stretch')
Inputs may be any that keep to these rules, and one draw needn't show every extreme that they name: ancestry describes a tree rooted at segment 0 in which every segment's parent has a lower number: entry [a, b] is 1 exactly when b is a or an ancestor of a.
All inputs are finite; a program needn't handle non-finite values.
Results may differ from a plain program's by a relative error of at most 0.0085.
Values may be sent and summed in bfloat16 or wider, within the bound.
A program may use at most 64 MiB of HBM per device.

v0:
```python
import math

import jax
import jax.numpy as jnp
from jax import lax
from jax.sharding import PartitionSpec as P

HEADS = 64
KV_HEADS = 8
HEAD_DIM = 128


lowest = -1e30


def passed_along(value, axis, steps):
    count = lax.axis_size(axis)
    pairs = [(source, (source + steps) % count) for source in range(count)]
    return lax.ppermute(value, axis, pairs)


def attend(query_rows, key_rows, value_rows, allowed):
    scores = jnp.einsum("pgrd,ngd->pgrn", query_rows, key_rows, preferred_element_type=jnp.float32)
    scores = scores * (1.0 / math.sqrt(query_rows.shape[-1]))
    visible = allowed[:, None, None, :]
    scores = jnp.where(visible, scores, lowest)
    peak = jnp.max(scores, -1)
    weights = jnp.where(visible, jnp.exp(scores - peak[..., None]), 0.0)
    totals = jnp.sum(weights, -1)
    blended = jnp.einsum(
        "pgrn,ngd->pgrd",
        weights.astype(jnp.bfloat16),
        value_rows,
        preferred_element_type=jnp.float32,
    )
    return (peak, totals, blended)


def combine(former, latter):
    peak = jnp.maximum(former[0], latter[0])
    former_scale = jnp.exp(former[0] - peak)
    latter_scale = jnp.exp(latter[0] - peak)
    totals = former[1] * former_scale + latter[1] * latter_scale
    blended = former[2] * former_scale[..., None] + latter[2] * latter_scale[..., None]
    return (peak, totals, blended)


def local(queries, branch_kv, prompt_kv, ancestry, segment_of_slot, counts):
    row_count = queries.shape[0]
    features = queries.shape[1]
    per_dev = features // HEAD_DIM
    group_size = HEADS // KV_HEADS
    kv_per = max(1, per_dev // group_size)
    sub_heads = per_dev // kv_per
    local_prompt = prompt_kv.shape[1]
    prompt_pos = lax.axis_index("stretch")
    first_kv = prompt_pos * per_dev // group_size
    mine_q = queries.reshape(row_count, kv_per, sub_heads, HEAD_DIM)
    empty_state = (
        jnp.full((row_count, kv_per, sub_heads), lowest, jnp.float32),
        jnp.zeros((row_count, kv_per, sub_heads), jnp.float32),
        jnp.zeros((row_count, kv_per, sub_heads, HEAD_DIM), jnp.float32),
    )
    incoming = lax.all_gather(prompt_kv, "stretch", axis=1, tiled=True)
    incoming_rows = incoming.shape[1]
    pieces = incoming_rows // local_prompt
    sliced = lax.dynamic_slice_in_dim(incoming, first_kv * HEAD_DIM, kv_per * HEAD_DIM, 2)
    key_blocks = sliced[0].reshape(pieces, local_prompt, kv_per, HEAD_DIM)
    value_blocks = sliced[1].reshape(pieces, local_prompt, kv_per, HEAD_DIM)
    open_keys = jnp.ones((1, local_prompt), dtype=bool)

    def piece_step(state_now, blocks_now):
        return (combine(state_now, attend(mine_q, blocks_now[0], blocks_now[1], open_keys)), None)

    result, unused = lax.scan(piece_step, empty_state, (key_blocks, value_blocks))
    status = result
    my_slot = lax.axis_index("seg")
    seg_count = lax.axis_size("seg")
    my_segment = segment_of_slot[my_slot]
    positions = jnp.arange(row_count, dtype=jnp.int32)
    own_kv = lax.dynamic_slice_in_dim(branch_kv, first_kv * HEAD_DIM, kv_per * HEAD_DIM, 2)

    def branch_step(carry_state, kv_block, source, enabled):
        segment = segment_of_slot[source]
        linked = (ancestry[my_segment, segment] > 0) & enabled
        live = positions < counts[segment]
        allowed = live[None, :] & ((source != my_slot) | (positions[None, :] <= positions[:, None]))

        def work(state_now):
            key_rows = kv_block[0].reshape(row_count, kv_per, HEAD_DIM)
            value_rows = kv_block[1].reshape(row_count, kv_per, HEAD_DIM)
            return combine(state_now, attend(mine_q, key_rows, value_rows, allowed))

        def unchanged(state_now):
            return state_now

        return lax.cond(linked, work, unchanged, carry_state)

    status = branch_step(status, own_kv, my_slot, jnp.asarray(True))

    def hop_single(hop_index, carry):
        moving, state_now = carry
        moving = passed_along(moving, "seg", 1)
        source = (my_slot - hop_index) % seg_count
        return (moving, branch_step(state_now, moving, source, jnp.asarray(True)))

    status = lax.fori_loop(1, seg_count, hop_single, (own_kv, status))[1]
    result = status[2] / status[1][..., None]
    return result.reshape(row_count, features).astype(jnp.bfloat16)


def solution(mesh):
    return jax.shard_map(
        local,
        mesh=mesh,
        in_specs=(
            P("seg", "stretch"),
            P(None, "seg", None),
            P(None, "stretch", None),
            P(),
            P(),
            P(),
        ),
        out_specs=P("seg", "stretch"),
        check_vma=False,
    )
```

profile of v0, /device:TPU:0, one launch (start us, length us, event | category | flops | bytes accessed | tf_op | source)
XLA Modules:
  0.0 159.6 jit_solution(5563451975604316101)
XLA Ops:
  6.5 0.7 all-gather.2.cloned.1.call-update
  7.3 1.3 dynamic_slice.54
  9.9 1.3 copy.19
  11.2 0.3 copy.21
  11.6 0.7 copy.47
  13.0 1.3 dynamic_slice.55
  14.9 60.2 %all-gather.2.cloned.1.call-done = bf16[2,768,1024]{2,1,0:T(8,128)(2,1)} async-done(((bf16[2,192,1024]{2,1,0:T(8,128)(2,1)}), bf16[2,768,1024]{2,1,0:T(8,128)(2,1)}) %all-gather.2.cloned.1.call-update) | async-done | bytes 3145744 | tf_op jit(solution)/shard_map/all_gather | solution.py:64
  75.1 1.2 constant_dynamic-slice_fusion.3
  76.5 12.5 %while.39 = (s32[]{:T(128)}, f32[128,2,8]{0,2,1:T(8,128)S(1)}, f32[128,2,8]{0,2,1:T(8,128)S(1)}, f32[128,2,8,128]{0,3,2,1:T(8,128)}, bf16[4,192,2,128]{3,2,1,0:T...) while((s32[]{:T(128)}, f32[128,2,8]{0,2,1:T(8,128)S(1)}, ...), condition=%wide.region_3.4_spmd.clone, body=%wide.region_0.3_spmd.clone.sunk | while | flops 204746752 | bytes 8044652 | solution.py:75
  76.5 0.1 constant_dynamic-slice_fusion.6
  76.7 0.4 bitcast_reduce_fusion.2
  77.1 0.2 fusion.50
  77.3 1.4 fusion.52
  78.8 0.1 constant_dynamic-slice_fusion.6
  78.9 0.4 bitcast_reduce_fusion.2
  79.3 0.2 fusion.50
  79.5 2.6 %fusion.52 = f32[128,2,8,128]{0,3,2,1:T(8,128)} fusion(f32[128,2,8,128]{0,3,2,1:T(8,128)} %get-tuple-element.804, f32[2,192,128,8]{2,1,3,0:T(8,128)S(1)} %get-tuple-element.779, f32[128,2,8]{0,2,1:T(8,128)S(1)} %get-tuple-element.780, f32[128,2,8]{0,2,1:T(8,128)S(1)} %get-tuple-element.783, f32[128,2,8]{0,2,1:T(8,128)S(1)} %get-tuple-element.784, ...), kind=kOutput, calls=%fused_computation.45.clone.1 | convolution fusion | flops 102498304 | bytes 3792897 | tf_op jit(solution)/shard_map/while/body/eval_jaxpr/pgrn,ngd->pgrd/dot_general | solution.py:30
  82.3 0.4 bitcast_reduce_fusion.2
  82.7 0.2 fusion.50
  83.0 2.6 %fusion.52 = f32[128,2,8,128]{0,3,2,1:T(8,128)} fusion(f32[128,2,8,128]{0,3,2,1:T(8,128)} %get-tuple-element.804, f32[2,192,128,8]{2,1,3,0:T(8,128)S(1)} %get-tuple-element.779, f32[128,2,8]{0,2,1:T(8,128)S(1)} %get-tuple-element.780, f32[128,2,8]{0,2,1:T(8,128)S(1)} %get-tuple-element.783, f32[128,2,8]{0,2,1:T(8,128)S(1)} %get-tuple-element.784, ...), kind=kOutput, calls=%fused_computation.45.clone.1 | convolution fusion | flops 102498304 | bytes 3792897 | tf_op jit(solution)/shard_map/while/body/eval_jaxpr/pgrn,ngd->pgrd/dot_general | solution.py:30
  85.6 0.1 constant_dynamic-slice_fusion.6
  85.8 0.4 bitcast_reduce_fusion.2
  86.2 0.2 fusion.50
  86.4 2.6 %fusion.52 = f32[128,2,8,128]{0,3,2,1:T(8,128)} fusion(f32[128,2,8,128]{0,3,2,1:T(8,128)} %get-tuple-element.804, f32[2,192,128,8]{2,1,3,0:T(8,128)S(1)} %get-tuple-element.779, f32[128,2,8]{0,2,1:T(8,128)S(1)} %get-tuple-element.780, f32[128,2,8]{0,2,1:T(8,128)S(1)} %get-tuple-element.783, f32[128,2,8]{0,2,1:T(8,128)S(1)} %get-tuple-element.784, ...), kind=kOutput, calls=%fused_computation.45.clone.1 | convolution fusion | flops 102498304 | bytes 3792897 | tf_op jit(solution)/shard_map/while/body/eval_jaxpr/pgrn,ngd->pgrd/dot_general | solution.py:30
  89.1 7.3 %conditional.2 = (f32[128,2,8]{0,2,1:T(8,128)S(1)}, f32[128,2,8]{0,2,1:T(8,128)S(1)}, f32[128,2,8,128]{3,0,2,1:T(8,128)S(1)}) conditional(s32[]{:T(128)} %bitcast.16, (f32[128,2,8]{0,2,1:T(8,128)S(1)}, f32[128,2,8]{0,2,1:T(8,128)S(1)}, f32[128,2,8,128]{0,3,2,1:T(8,128)}) %tuple.46, (s32[8]{0:T(128)S(1)}, s32[]{:T(128)}, s32[1,128]{1,0:T(1,128)S(1)}, ...), branch_computations={%region_4.5_spmd, %region_5.8_spmd} | conditional | flops 137404544 | bytes 12763972 | solution.py:97
  89.1 0.6 dynamic_slice.45
  89.8 0.6 compare_bitcast_fusion
  90.5 1.0 fusion.32
  91.5 1.4 fusion.33
  92.9 0.2 fusion.7
  93.1 1.3 copy.25
  94.4 1.9 %fusion.3 = f32[128,2,8,128]{3,0,2,1:T(8,128)S(1)} fusion(bf16[128,2,128,1]{0,2,3,1:T(8,128)(2,1)S(1)} %bitcast.114, f32[128,2,8,128]{3,0,2,1:T(8,128)} %copy.25, f32[128,2,8,128]{0,3,2,1:T(8,128)S(1)} %get-tuple-element.643, f32[128,2,8]{0,2,1:T(8,128)S(1)} %get-tuple-element.630, f32[128,2,8]{0,2,1:T(8,128)S(1)} %get-tuple-element.629, ...), kind=kOutput, calls=%fused_computation.3 | convolution fusion | flops 68681728 | bytes 3252224 | tf_op jit(solution)/shard_map/cond/branch_1_fun/pgrn,ngd->pgrd/dot_general | solution.py:30
  96.4 54.7 %while.38 = (s32[]{:T(128)}, bf16[2,128,256]{1,2,0:T(8,128)(2,1)}, f32[128,2,8]{0,2,1:T(8,128)S(1)}, f32[128,2,8]{0,2,1:T(8,128)S(1)}, f32[128,2,8,128]{3,0,2,1:...) while((s32[]{:T(128)}, bf16[2,128,256]{1,2,0:T(8,128)(2,1)}, ...), condition=%wide.region_13.14_spmd.clone.clone, body=%wide.region_8.13_spmd.clone.clone.sunk | while | flops 137420944 | bytes 7129418 | solution.py:107
  96.5 0.6 dynamic_slice.69
  99.0 1.3 dynamic_slice.70
  101.0 1.0 collective-permute-done
  102.0 0.6 copy.96
  102.6 3.8 %collective-permute-start = (bf16[2,128,256]{1,2,0:T(8,128)(2,1)}, bf16[2,128,256]{1,2,0:T(8,128)(2,1)S(1)}, u32[]{:S(2)}, u32[]{:S(2)}) collective-permute-start(bf16[2,128,256]{1,2,0:T(8,128)(2,1)} %get-tuple-element.842), channel_id=1, source_target_pairs={{0,4},{4,8},{8,12},{12,16},{16,20},{20,24},{24,28},{28,0},{1,5},{5... | collective-permute-start | bytes 393224 | tf_op jit(solution)/shard_map/while/body/eval_jaxpr/ppermute | solution.py:19
  106.4 0.6 dynamic_slice.69
  108.9 1.3 dynamic_slice.70
  110.9 0.6 copy.96
  111.6 0.6 dynamic_slice.69
  114.1 1.3 dynamic_slice.70
  116.0 2.6 %collective-permute-done = bf16[2,128,256]{1,2,0:T(8,128)(2,1)S(1)} collective-permute-done((bf16[2,128,256]{1,2,0:T(8,128)(2,1)}, bf16[2,128,256]{1,2,0:T(8,128)(2,1)S(1)}, u32[]{:S(2)}, u32[]{:S(2)}) %collective-permute-start) | collective-permute-done | bytes 131104 | tf_op jit(solution)/shard_map/while/body/eval_jaxpr/ppermute | solution.py:19
  118.6 0.6 copy.96
  119.3 3.9 %collective-permute-start = (bf16[2,128,256]{1,2,0:T(8,128)(2,1)}, bf16[2,128,256]{1,2,0:T(8,128)(2,1)S(1)}, u32[]{:S(2)}, u32[]{:S(2)}) collective-permute-start(bf16[2,128,256]{1,2,0:T(8,128)(2,1)} %get-tuple-element.842), channel_id=1, source_target_pairs={{0,4},{4,8},{8,12},{12,16},{16,20},{20,24},{24,28},{28,0},{1,5},{5... | collective-permute-start | bytes 393224 | tf_op jit(solution)/shard_map/while/body/eval_jaxpr/ppermute | solution.py:19
  123.2 0.6 dynamic_slice.69
  125.7 1.3 dynamic_slice.70
  127.7 0.6 copy.96
  128.3 3.2 %collective-permute-start = (bf16[2,128,256]{1,2,0:T(8,128)(2,1)}, bf16[2,128,256]{1,2,0:T(8,128)(2,1)S(1)}, u32[]{:S(2)}, u32[]{:S(2)}) collective-permute-start(bf16[2,128,256]{1,2,0:T(8,128)(2,1)} %get-tuple-element.842), channel_id=1, source_target_pairs={{0,4},{4,8},{8,12},{12,16},{16,20},{20,24},{24,28},{28,0},{1,5},{5... | collective-permute-start | bytes 393224 | tf_op jit(solution)/shard_map/while/body/eval_jaxpr/ppermute | solution.py:19
  131.5 0.6 dynamic_slice.69
  134.0 1.3 dynamic_slice.70
  136.0 0.6 copy.96
  136.7 0.6 dynamic_slice.69
  139.2 1.3 dynamic_slice.70
  141.1 1.0 collective-permute-done
  142.2 0.6 copy.96
  142.8 0.6 dynamic_slice.69
  145.3 1.3 dynamic_slice.70
  147.3 3.2 %collective-permute-done = bf16[2,128,256]{1,2,0:T(8,128)(2,1)S(1)} collective-permute-done((bf16[2,128,256]{1,2,0:T(8,128)(2,1)}, bf16[2,128,256]{1,2,0:T(8,128)(2,1)S(1)}, u32[]{:S(2)}, u32[]{:S(2)}) %collective-permute-start) | collective-permute-done | bytes 131104 | tf_op jit(solution)/shard_map/while/body/eval_jaxpr/ppermute | solution.py:19
  150.5 0.6 copy.96
  151.2 0.3 divide_convert_fusion
  151.5 0.3 copy.27
  151.9 0.9 copy.56
  (48 shorter events, 0.7 us)
Async XLA Ops:
  6.5 5.0 %copy-start = (bf16[2,128,1024]{2,1,0:T(8,128)(2,1)S(1)}, bf16[2,128,1024]{2,1,0:T(8,128)(2,1)}, u32[]{:S(2)}) copy-start(bf16[2,128,1024]{2,1,0:T(8,128)(2,1)} %param.15) | copy-start | bytes 1572868
  6.5 68.6 %all-gather.2.cloned.1.call-start = ((), (), s32[]{:S(2)}) async-start(), calls=%async_computation | async-start | bytes 3932160 | tf_op jit(solution)/shard_map/all_gather | solution.py:64
  11.2 65.1 %copy-start.2 = (bf16[128,2048]{0,1:T(8,128)(2,1)}, bf16[128,2048]{0,1:T(8,128)(2,1)S(1)}, u32[]{:S(2)}) copy-start(bf16[128,2048]{0,1:T(8,128)(2,1)S(1)} %copy.19) | copy-start | bytes 1572868
  76.5 12.6 %copy-start.4 = (s32[8]{0:T(128)S(1)}, s32[8]{0:T(128)}, u32[]{:S(2)}) copy-start(s32[8]{0:T(128)} %param.19) | copy-start | bytes 100
  89.1 7.3 %copy-start.3 = (s32[8]{0:T(128)S(1)}, s32[8]{0:T(128)}, u32[]{:S(2)}) copy-start(s32[8]{0:T(128)} %param.18) | copy-start | bytes 100
  90.5 2.6 %copy-start.1 = (f32[128,2,8,128]{0,3,2,1:T(8,128)S(1)}, f32[128,2,8,128]{0,3,2,1:T(8,128)}, u32[]{:S(2)}) copy-start(f32[128,2,8,128]{0,3,2,1:T(8,128)} %get-tuple-element.580) | copy-start | bytes 3145732 | tf_op jit(solution)/shard_map/cond
  96.4 5.6 %collective-permute-start = (bf16[2,128,256]{1,2,0:T(8,128)(2,1)}, bf16[2,128,256]{1,2,0:T(8,128)(2,1)S(1)}, u32[]{:S(2)}, u32[]{:S(2)}) collective-permute-start(bf16[2,128,256]{1,2,0:T(8,128)(2,1)} %get-tuple-element.842), channel_id=1, source_target_pairs={{0,4},{4,8},{8,12},{12,16},{16,20},{20,24},{24,28},{28,0},{1,5},{5... | collective-permute-start | bytes 393224 | tf_op jit(solution)/shard_map/while/body/eval_jaxpr/ppermute | solution.py:19
  102.6 8.3 %collective-permute-start = (bf16[2,128,256]{1,2,0:T(8,128)(2,1)}, bf16[2,128,256]{1,2,0:T(8,128)(2,1)S(1)}, u32[]{:S(2)}, u32[]{:S(2)}) collective-permute-start(bf16[2,128,256]{1,2,0:T(8,128)(2,1)} %get-tuple-element.842), channel_id=1, source_target_pairs={{0,4},{4,8},{8,12},{12,16},{16,20},{20,24},{24,28},{28,0},{1,5},{5... | collective-permute-start | bytes 393224 | tf_op jit(solution)/shard_map/while/body/eval_jaxpr/ppermute | solution.py:19
  111.6 7.1 %collective-permute-start = (bf16[2,128,256]{1,2,0:T(8,128)(2,1)}, bf16[2,128,256]{1,2,0:T(8,128)(2,1)S(1)}, u32[]{:S(2)}, u32[]{:S(2)}) collective-permute-start(bf16[2,128,256]{1,2,0:T(8,128)(2,1)} %get-tuple-element.842), channel_id=1, source_target_pairs={{0,4},{4,8},{8,12},{12,16},{16,20},{20,24},{24,28},{28,0},{1,5},{5... | collective-permute-start | bytes 393224 | tf_op jit(solution)/shard_map/while/body/eval_jaxpr/ppermute | solution.py:19
  119.3 8.4 %collective-permute-start = (bf16[2,128,256]{1,2,0:T(8,128)(2,1)}, bf16[2,128,256]{1,2,0:T(8,128)(2,1)S(1)}, u32[]{:S(2)}, u32[]{:S(2)}) collective-permute-start(bf16[2,128,256]{1,2,0:T(8,128)(2,1)} %get-tuple-element.842), channel_id=1, source_target_pairs={{0,4},{4,8},{8,12},{12,16},{16,20},{20,24},{24,28},{28,0},{1,5},{5... | collective-permute-start | bytes 393224 | tf_op jit(solution)/shard_map/while/body/eval_jaxpr/ppermute | solution.py:19
  128.3 7.6 %collective-permute-start = (bf16[2,128,256]{1,2,0:T(8,128)(2,1)}, bf16[2,128,256]{1,2,0:T(8,128)(2,1)S(1)}, u32[]{:S(2)}, u32[]{:S(2)}) collective-permute-start(bf16[2,128,256]{1,2,0:T(8,128)(2,1)} %get-tuple-element.842), channel_id=1, source_target_pairs={{0,4},{4,8},{8,12},{12,16},{16,20},{20,24},{24,28},{28,0},{1,5},{5... | collective-permute-start | bytes 393224 | tf_op jit(solution)/shard_map/while/body/eval_jaxpr/ppermute | solution.py:19
  136.7 5.5 %collective-permute-start = (bf16[2,128,256]{1,2,0:T(8,128)(2,1)}, bf16[2,128,256]{1,2,0:T(8,128)(2,1)S(1)}, u32[]{:S(2)}, u32[]{:S(2)}) collective-permute-start(bf16[2,128,256]{1,2,0:T(8,128)(2,1)} %get-tuple-element.842), channel_id=1, source_target_pairs={{0,4},{4,8},{8,12},{12,16},{16,20},{20,24},{24,28},{28,0},{1,5},{5... | collective-permute-start | bytes 393224 | tf_op jit(solution)/shard_map/while/body/eval_jaxpr/ppermute | solution.py:19
  142.8 7.7 %collective-permute-start = (bf16[2,128,256]{1,2,0:T(8,128)(2,1)}, bf16[2,128,256]{1,2,0:T(8,128)(2,1)S(1)}, u32[]{:S(2)}, u32[]{:S(2)}) collective-permute-start(bf16[2,128,256]{1,2,0:T(8,128)(2,1)} %get-tuple-element.842), channel_id=1, source_target_pairs={{0,4},{4,8},{8,12},{12,16},{16,20},{20,24},{24,28},{28,0},{1,5},{5... | collective-permute-start | bytes 393224 | tf_op jit(solution)/shard_map/while/body/eval_jaxpr/ppermute | solution.py:19
Sparse Core Ops, SparseCore 0:
  8.9 66.1 all-gather.1
where the time goes:
time: 161 us; the launch traced here: 160 us
  waiting for transfers between devices  68.8 us (43%)
  local copies, waits for them, and re-layouts  29.1 us (18%)
  loops' own time  18.2 us (11%)
  between operations  16.1 us (10%)
  matrix products  14.2 us (9%)
  starting transfers between devices  11 us (7%)
  other arithmetic  2.25 us (1%)
    all_gather x1, waiting for transfers between devices, local(): incoming = lax.all_gather(prompt_kv, 'stretch', axis=1, tiled=True)  60.2 us
    another operation x1, loops' own time, local(): status = lax.fori_loop(1, seg_count, hop_single, (own_kv, status))[1]  18 us
    dot_general x5, matrix products, attend(): jnp.einsum('pgrn,ngd->pgrd', weights.astype(jnp.bfloat16), value_rows, pr...  11.3 us
    ppermute x7, starting transfers between devices, passed_along(): return lax.ppermute(value, axis, pairs)  11 us
    dynamic_slice x8, local copies, waits for them, and re-layouts, branch_step(): linked = (ancestry[my_segment, segment] > 0) & enabled  10.5 us
    ppermute x7, waiting for transfers between devices, passed_along(): return lax.ppermute(value, axis, pairs)  7.88 us
    while x7, local copies, waits for them, and re-layouts  4.51 us
    dynamic_slice x7, local copies, waits for them, and re-layouts, branch_step(): segment = segment_of_slot[source]  4.25 us
  transfers between devices with their start and end apart: 8, of which 5 were waited for; matrix products, arithmetic and copies ran while one was open for 12% of the time, Pallas kernels for 0%

commit v1 on v0

v1 whole, which is shorter than its diff:
```python
import functools
import math

import jax
import jax.numpy as jnp
from jax import lax
from jax.experimental import pallas as pl
from jax.experimental.pallas import tpu as pltpu
from jax.sharding import PartitionSpec as P

HEADS = 64
KV_HEADS = 8
HEAD_DIM = 128
GROUP = HEADS // KV_HEADS
CUBE = 8
EXP2_SCALE = math.log2(math.e) / math.sqrt(HEAD_DIM)
HIDDEN = -1e30

OWN, SIB, A, B, SIB_A, SIB_B, DIAG, SIB_DIAG = range(8)


def kernel(
    seg_count, stretch_count, block_rows,
    anc_ref, seg_ref, cnt_ref, q_hbm, branch_hbm, prompt_hbm, out_ref,
    q_ref, own_prompt, branch, prompt, peak_ref, acc_ref, tot_ref,
    local_sem, z_send, z_recv, g_send, g_recv, b_send, b_recv, p_send, p_recv,
):
    per_dev = q_hbm.shape[1] // HEAD_DIM
    rows = q_hbm.shape[0]
    kv_per = max(1, per_dev // GROUP)
    sub = per_dev // kv_per
    width = kv_per * HEAD_DIM
    groups = seg_count // CUBE
    part = prompt_hbm.shape[1] // (CUBE // 2)

    s = lax.axis_index("seg")
    z = lax.axis_index("stretch")
    g, r = s // CUBE, s % CUBE
    chip, c = r // 2, r % 2
    y, x = r // 4, (r // 2) % 2
    dx, dy, dc = 2 - 4 * x, 4 - 8 * y, 1 - 2 * c
    da = (1 - c) * dx + c * dy
    db = c * dx + (1 - c) * dy
    to_a, to_b, to_sib = {"seg": s + da}, {"seg": s + db}, {"seg": s + dc}
    at_a, at_b = 1 + c, 2 - c

    def columns(stretch):
        first = stretch * per_dev // GROUP
        return pl.ds(pl.multiple_of(first * HEAD_DIM, HEAD_DIM), width)

    loads = [
        pltpu.make_async_copy(q_hbm, q_ref, local_sem.at[0]),
        pltpu.make_async_copy(branch_hbm.at[:, :, columns(z)], branch.at[OWN, 0], local_sem.at[1]),
        pltpu.make_async_copy(prompt_hbm.at[:, :, columns(z)], own_prompt, local_sem.at[2]),
    ]
    barrier = pltpu.get_barrier_semaphore()
    partners = [to_a, to_b, to_sib]
    partners += [{"stretch": (z + j) % stretch_count} for j in range(1, stretch_count)]
    partners += [{"seg": (g + j) % groups * CUBE + r} for j in range(1, groups)]
    for partner in partners:
        pl.semaphore_signal(barrier, inc=1, device_id=partner, device_id_type=pl.DeviceIdType.MESH)
    for load in loads:
        load.start()
    pl.semaphore_wait(barrier, len(partners))

    sent = []

    def send(source, target, send_sem, recv_sem, device):
        copy = pltpu.make_async_remote_copy(
            src_ref=source, dst_ref=target, send_sem=send_sem, recv_sem=recv_sem,
            device_id=device, device_id_type=pl.DeviceIdType.MESH,
        )
        copy.start()
        sent.append(copy)

    def arrived(target, recv_sem):
        pltpu.make_async_copy(target, target, recv_sem).wait()

    quarter = pl.ds(pl.multiple_of(chip * part, 16), part)
    for j in range(1, stretch_count):
        other = (z + stretch_count - j) % stretch_count
        send(
            prompt_hbm.at[c, quarter, columns(other)], prompt.at[c, 0, j - 1],
            z_send.at[j - 1], z_recv.at[j - 1], {"stretch": other},
        )
    for j in range(1, groups):
        send(
            branch_hbm.at[:, :, columns(z)], branch.at[OWN, j],
            g_send.at[j - 1], g_recv.at[j - 1], {"seg": (g + groups - j) % groups * CUBE + r},
        )
    if groups > 1:
        loads[1].wait()
        for j in range(1, groups):
            arrived(branch.at[OWN, j], g_recv.at[j - 1])

    def branch_part(slot, kind):
        return branch.at[slot, :, kind]

    def send_branch(slot, kind, target, device):
        if groups == 1 and slot == OWN:
            source = branch_hbm.at[kind, :, columns(z)]
            place = branch.at[target, 0, kind]
        else:
            source, place = branch_part(slot, kind), branch_part(target, kind)
        send(source, place, b_send.at[target, kind], b_recv.at[target, kind], device)

    def branch_arrived(slot, kind):
        arrived(branch_part(slot, kind), b_recv.at[slot, kind])

    for kind in range(2):
        send_branch(OWN, kind, A, to_a)
        send_branch(OWN, kind, SIB, to_sib)
    for kind in range(2):
        send_branch(OWN, kind, B, to_b)

    def send_prompt(place, target_place, message, device):
        send(prompt.at[c, place], prompt.at[c, target_place], p_send.at[message], p_recv.at[message], device)

    def prompt_arrived(kind, place, message):
        arrived(prompt.at[kind, place], p_recv.at[message])

    def linked_rows(rank, j):
        slot = (g + j) % groups * CUBE + rank
        segment = seg_ref[slot]
        return anc_ref[seg_ref[s], segment] * cnt_ref[segment]

    ranks = {
        OWN: r, SIB: r + dc, A: r + da, B: r + db, SIB_A: r + dc + db, SIB_B: r + dc + da,
        DIAG: r + da + db, SIB_DIAG: r + dc + da + db,
    }
    ones = jnp.ones((1, HEAD_DIM), jnp.float32)

    def operands(slots, h):
        cols = slice(h * HEAD_DIM, (h + 1) * HEAD_DIM)
        first_key = own_prompt[0, 0:16, cols].astype(jnp.float32)[0:1]
        keys, values = [], []
        place = lax.broadcasted_iota(jnp.int32, (rows, HEAD_DIM), 0)
        for slot in slots:
            for j in range(groups):
                live = place < linked_rows(ranks[slot], j)
                key = branch[slot, j, 0, :, cols].astype(jnp.float32)
                value = branch[slot, j, 1, :, cols].astype(jnp.float32)
                keys.append(jnp.where(live, key, first_key).astype(jnp.bfloat16))
                values.append(
                    jnp.concatenate([jnp.where(live, value, 0.0), jnp.where(live, 1.0, 0.0)], 1).astype(jnp.bfloat16)
                )
        return jnp.concatenate(keys, 0), jnp.concatenate(values, 0)

    def prompt_operands(h):
        cols = slice(h * HEAD_DIM, (h + 1) * HEAD_DIM)
        count = (CUBE // 2) * (stretch_count - 1) * part
        out = []
        for kind in range(2):
            out.append(jnp.concatenate([own_prompt[kind, :, cols], prompt[kind, :, :, :, cols].reshape(count, HEAD_DIM)], 0))
        keys, values = out
        return keys, jnp.concatenate([values, jnp.ones_like(values)], 1)

    def attend(h, keys, values, first=False, last=False):
        count = keys.shape[0]
        heads = block_rows // rows
        for start in range(0, sub, heads):
            span = slice(start * rows, (start + heads) * rows)
            query = jnp.concatenate(
                [q_ref[:, (h * sub + i) * HEAD_DIM:(h * sub + i + 1) * HEAD_DIM] for i in range(start, start + heads)], 0
            )
            scores = lax.dot_general(query, keys, (((1,), (1,)), ((), ())), preferred_element_type=jnp.float32)
            tiles = [scores[:, t:t + HEAD_DIM] for t in range(0, count, HEAD_DIM)]
            if first:
                causal = lax.broadcasted_iota(jnp.int32, (block_rows, HEAD_DIM), 1) <= (
                    lax.broadcasted_iota(jnp.int32, (block_rows, HEAD_DIM), 0) % rows
                )
                tiles[0] = jnp.where(causal, tiles[0], HIDDEN)
            top = functools.reduce(jnp.maximum, tiles)
            peak = jnp.max(top, -1, keepdims=True)
            if first:
                peak = jnp.broadcast_to(peak, (block_rows, HEAD_DIM))
            else:
                former = peak_ref[h, span]
                peak = jnp.maximum(former, peak)
            weights = jnp.concatenate([jnp.exp2((tile - peak) * EXP2_SCALE).astype(jnp.bfloat16) for tile in tiles], 1)
            both = lax.dot_general(weights, values, (((1,), (0,)), ((), ())), preferred_element_type=jnp.float32)
            acc, tot = both[:, :HEAD_DIM], both[:, HEAD_DIM:]
            if not first:
                scale = jnp.exp2((former - peak) * EXP2_SCALE)
                acc = acc + acc_ref[h, span] * scale
                tot = tot + tot_ref[h, span] * scale
            if last:
                result = (acc / tot).astype(jnp.bfloat16)
                for i in range(heads):
                    head = h * sub + start + i
                    out_ref[:, head * HEAD_DIM:(head + 1) * HEAD_DIM] = result[i * rows:(i + 1) * rows]
            else:
                peak_ref[h, span] = peak
                acc_ref[h, span] = acc
                tot_ref[h, span] = tot

    loads[0].wait()
    if groups == 1:
        loads[1].wait()
    loads[2].wait()
    for kind in range(2):
        branch_arrived(SIB, kind)
    for h in range(kv_per):
        attend(h, *operands([OWN, SIB] if groups == 1 else [OWN], h), first=True)
    for j in range(1, stretch_count):
        arrived(prompt.at[c, 0, j - 1], z_recv.at[j - 1])
    send_prompt(0, at_a, 0, to_a)
    send_prompt(0, at_b, 1, to_b)
    send_prompt(0, 0, 3, to_sib)
    for kind in range(2):
        branch_arrived(A, kind)
        send_branch(A, kind, DIAG, to_b)
        send_branch(A, kind, SIB_A, to_sib)
    for kind in range(2):
        branch_arrived(B, kind)
        send_branch(B, kind, SIB_B, to_sib)
    for slot in (SIB_A, SIB_B):
        for kind in range(2):
            branch_arrived(slot, kind)
    near = [A, B, SIB_A, SIB_B]
    if groups > 1:
        near = [SIB] + near
    attend(0, *operands(near, 0))
    prompt_arrived(c, at_a, 0)
    send_prompt(at_a, 3, 2, to_b)
    send_prompt(at_a, at_a, 4, to_sib)
    prompt_arrived(c, at_b, 1)
    send_prompt(at_b, at_b, 5, to_sib)
    for kind in range(2):
        branch_arrived(DIAG, kind)
        send_branch(DIAG, kind, SIB_DIAG, to_sib)
    for h in range(1, kv_per):
        attend(h, *operands(near, h))
    prompt_arrived(c, 3, 2)
    send_prompt(3, 3, 6, to_sib)
    for kind in range(2):
        branch_arrived(SIB_DIAG, kind)
    for h in range(kv_per):
        attend(h, *operands([DIAG, SIB_DIAG], h))
    prompt_arrived(1 - c, 0, 3)
    prompt_arrived(1 - c, at_b, 4)
    prompt_arrived(1 - c, at_a, 5)
    prompt_arrived(1 - c, 3, 6)
    for h in range(kv_per):
        attend(h, *prompt_operands(h), last=True)
    for copy in sent:
        copy.wait_send()


def local(queries, branch_kv, prompt_kv, ancestry, segment_of_slot, counts):
    seg_count = lax.axis_size("seg")
    stretch_count = lax.axis_size("stretch")
    rows, features = queries.shape
    per_dev = features // HEAD_DIM
    kv_per = max(1, per_dev // GROUP)
    sub = per_dev // kv_per
    width = kv_per * HEAD_DIM
    groups = seg_count // CUBE
    part = prompt_kv.shape[1] // (CUBE // 2)
    state = pltpu.VMEM((kv_per, sub * rows, HEAD_DIM), jnp.float32)
    dma = pltpu.SemaphoreType.DMA
    smem = pl.BlockSpec(memory_space=pltpu.SMEM)
    hbm = pl.BlockSpec(memory_space=pl.ANY)
    return pl.pallas_call(
        functools.partial(kernel, seg_count, stretch_count, min(sub, 4) * rows),
        out_shape=jax.ShapeDtypeStruct((rows, features), jnp.bfloat16),
        in_specs=[smem, smem, smem, hbm, hbm, hbm],
        out_specs=pl.BlockSpec(memory_space=pltpu.VMEM),
        scratch_shapes=[
            pltpu.VMEM((rows, features), jnp.bfloat16),
            pltpu.VMEM((2, prompt_kv.shape[1], width), jnp.bfloat16),
            pltpu.VMEM((CUBE, groups, 2, rows, width), jnp.bfloat16),
            pltpu.VMEM((2, CUBE // 2, stretch_count - 1, part, width), jnp.bfloat16),
            state, state, state,
            dma((3,)),
            dma((stretch_count - 1,)), dma((stretch_count - 1,)),
            dma((max(1, groups - 1),)), dma((max(1, groups - 1),)),
            dma((8, 2)), dma((8, 2)),
            dma((7,)), dma((7,)),
        ],
        compiler_params=pltpu.CompilerParams(
            collective_id=0, has_side_effects=True, vmem_limit_bytes=40 * 1024 * 1024
        ),
    )(ancestry, segment_of_slot, counts, queries, branch_kv, prompt_kv)


def solution(mesh):
    return jax.shard_map(
        local,
        mesh=mesh,
        in_specs=(
            P("seg", "stretch"),
            P(None, "seg", None),
            P(None, "stretch", None),
            P(),
            P(),
            P(),
        ),
        out_specs=P("seg", "stretch"),
        check_vma=False,
    )
```

time: 161 us -> 27.6 us (0.17)
  waiting for transfers between devices: 68.8 us -> 0 us
  local copies, waits for them, and re-layouts: 29.1 us -> 6.01 us
  Pallas kernels: 0 us -> 21.3 us
  loops' own time: 18.2 us -> 0 us
  between operations: 16.1 us -> 0.02 us
  matrix products: 14.2 us -> 0 us
  starting transfers between devices: 11 us -> 0 us
  other arithmetic: 2.25 us -> 0 us
    all_gather x1 -> x0, waiting for transfers between devices: 60.2 us -> none  [local(): incoming = lax.all_gather(prompt_kv, 'stretch', axis=1, tiled=True)]
    pallas_call x0 -> x1, Pallas kernels: none -> 21.3 us  [local(): pl.pallas_call(functools.partial(kernel, seg_count, stretch_count, min(su...]
    another operation x10 -> x0, loops' own time: 18.2 us -> none  [the longest x1 18 us: local(): status = lax.fori_loop(1, seg_count, hop_single, (own_kv, status))[1]]
    dynamic_slice x22 -> x0, local copies, waits for them, and re-layouts: 17.2 us -> none  [the longest x8 10.5 us: branch_step(): linked = (ancestry[my_segment, segment] > 0) & enabled]
    dot_general x10 -> x0, matrix products: 14.2 us -> none  [the longest x5 11.3 us: attend(): jnp.einsum('pgrn,ngd->pgrd', weights.astype(jnp.bfloat16), value_rows, pr...]
    ppermute x7 -> x0, starting transfers between devices: 11 us -> none  [passed_along(): return lax.ppermute(value, axis, pairs)]
    ppermute x7 -> x0, waiting for transfers between devices: 7.88 us -> none  [passed_along(): return lax.ppermute(value, axis, pairs)]
    while x7 -> x0, local copies, waits for them, and re-layouts: 4.51 us -> none
  transfers between devices with their start and end apart: 8 -> 0, of which waited for: 5 -> 0; matrix products, arithmetic and copies ran while one was open for 12% -> 0% of each run, Pallas kernels for 0% -> 0%
where the time goes in v1:
time: 27.6 us; the launch traced here: 27.3 us
  Pallas kernels  21.3 us (77%)
  local copies, waits for them, and re-layouts  6.01 us (22%)
    pallas_call x1, Pallas kernels, local(): pl.pallas_call(functools.partial(kernel, seg_count, stretch_count, min(su...  21.3 us
    unnamed x13, local copies, waits for them, and re-layouts  6.01 us

profile of v1, /device:TPU:0, one launch (start us, length us, event | category | flops | bytes accessed | tf_op | source)
XLA Modules:
  0.0 27.3 jit_solution(15405533490456079415)
XLA Ops:
  0.0 0.0 copy-start
  0.0 1.1 %copy-done = bf16[2,192,1024]{2,1,0:T(8,128)(2,1)S(1)} copy-done((bf16[2,192,1024]{2,1,0:T(8,128)(2,1)S(1)}, bf16[2,192,1024]{2,1,0:T(8,128)(2,1)}, u32[]{:S(2)}) %copy-start) | copy-done | bytes 786456
  1.1 0.0 copy-start.1
  1.1 1.0 %copy-done.1 = bf16[128,2048]{1,0:T(8,128)(2,1)S(1)} copy-done((bf16[128,2048]{1,0:T(8,128)(2,1)S(1)}, bf16[128,2048]{1,0:T(8,128)(2,1)}, u32[]{:S(2)}) %copy-start.1) | copy-done | bytes 524312
  2.2 0.0 copy-start.2
  2.2 1.0 %copy-done.2 = bf16[2,128,1024]{2,1,0:T(8,128)(2,1)S(1)} copy-done((bf16[2,128,1024]{2,1,0:T(8,128)(2,1)S(1)}, bf16[2,128,1024]{2,1,0:T(8,128)(2,1)}, u32[]{:S(2)}) %copy-start.2) | copy-done | bytes 524312
  3.2 0.0 copy-start.3
  3.2 0.7 %copy-done.3 = s32[8,8]{1,0:T(8,128)S(1)} copy-done((s32[8,8]{1,0:T(8,128)S(1)}, s32[8,8]{1,0:T(8,128)}, u32[]{:S(2)}) %copy-start.3) | copy-done | bytes 280
  3.9 0.0 copy-start.4
  3.9 0.7 %copy-done.4 = s32[8]{0:T(128)S(1)} copy-done((s32[8]{0:T(128)S(1)}, s32[8]{0:T(128)}, u32[]{:S(2)}) %copy-start.4) | copy-done | bytes 56
  4.6 0.0 copy-start.5
  4.6 0.7 %copy-done.5 = s32[8]{0:T(128)S(1)} copy-done((s32[8]{0:T(128)S(1)}, s32[8]{0:T(128)}, u32[]{:S(2)}) %copy-start.5) | copy-done | bytes 56
  5.2 21.3 %shard_map.64 = bf16[128,2048]{1,0:T(8,128)(2,1)S(1)} custom-call(s32[8,8]{1,0:T(8,128)S(1)} %copy-done.3, s32[8]{0:T(128)S(1)} %copy-done.4, s32[8]{0:T(128)S(1)} %copy-done.5, bf16[128,2048]{1,0:T(8,128)(2,1)S(1)} %copy-done.1, bf16[2,128,1024]{2,1,0:T(8,128)(2,1)S(1)} %copy-done.2, bf16[2,192,1024]{2,1,0:T(8,128)(2,1)S(1)} %copy-done), custom_call_target="tpu_custom_call" | custom-call | tf_op jit(solution)/shard_map/pallas_call | solution.py:264
  26.5 0.8 %copy.8 = bf16[128,2048]{1,0:T(8,128)(2,1)} copy(bf16[128,2048]{1,0:T(8,128)(2,1)S(1)} %shard_map.64) | data formatting | bytes 1048576
Async XLA Ops:
  0.0 1.1 %copy-start = (bf16[2,192,1024]{2,1,0:T(8,128)(2,1)S(1)}, bf16[2,192,1024]{2,1,0:T(8,128)(2,1)}, u32[]{:S(2)}) copy-start(bf16[2,192,1024]{2,1,0:T(8,128)(2,1)} %prompt_hbm.1) | copy-start | bytes 2359300
  1.1 1.0 %copy-start.1 = (bf16[128,2048]{1,0:T(8,128)(2,1)S(1)}, bf16[128,2048]{1,0:T(8,128)(2,1)}, u32[]{:S(2)}) copy-start(bf16[128,2048]{1,0:T(8,128)(2,1)} %q_hbm.1) | copy-start | bytes 1572868
  2.2 1.0 %copy-start.2 = (bf16[2,128,1024]{2,1,0:T(8,128)(2,1)S(1)}, bf16[2,128,1024]{2,1,0:T(8,128)(2,1)}, u32[]{:S(2)}) copy-start(bf16[2,128,1024]{2,1,0:T(8,128)(2,1)} %branch_hbm.1) | copy-start | bytes 1572868
  3.2 0.7 %copy-start.3 = (s32[8,8]{1,0:T(8,128)S(1)}, s32[8,8]{1,0:T(8,128)}, u32[]{:S(2)}) copy-start(s32[8,8]{1,0:T(8,128)} %anc_ref.1) | copy-start | bytes 772
  3.9 0.7 %copy-start.4 = (s32[8]{0:T(128)S(1)}, s32[8]{0:T(128)}, u32[]{:S(2)}) copy-start(s32[8]{0:T(128)} %seg_ref.1) | copy-start | bytes 100
  4.6 0.7 %copy-start.5 = (s32[8]{0:T(128)S(1)}, s32[8]{0:T(128)}, u32[]{:S(2)}) copy-start(s32[8]{0:T(128)} %cnt_ref.1) | copy-start | bytes 100

commit v2 on v1

--- a/solution.py
+++ b/solution.py
@@ -21,7 +21,8 @@
 
 def kernel(
     seg_count, stretch_count, block_rows,
-    anc_ref, seg_ref, cnt_ref, q_hbm, branch_hbm, prompt_hbm, out_ref,
+    anc_hbm, seg_hbm, cnt_hbm, q_hbm, branch_hbm, prompt_hbm, out_ref,
+    anc_ref, seg_ref, cnt_ref,
     q_ref, own_prompt, branch, prompt, peak_ref, acc_ref, tot_ref,
     local_sem, z_send, z_recv, g_send, g_recv, b_send, b_recv, p_send, p_recv,
 ):
@@ -31,18 +32,17 @@
     sub = per_dev // kv_per
     width = kv_per * HEAD_DIM
     groups = seg_count // CUBE
-    part = prompt_hbm.shape[1] // (CUBE // 2)
 
     s = lax.axis_index("seg")
     z = lax.axis_index("stretch")
     g, r = s // CUBE, s % CUBE
-    chip, c = r // 2, r % 2
+    c = r % 2
     y, x = r // 4, (r // 2) % 2
     dx, dy, dc = 2 - 4 * x, 4 - 8 * y, 1 - 2 * c
     da = (1 - c) * dx + c * dy
     db = c * dx + (1 - c) * dy
     to_a, to_b, to_sib = {"seg": s + da}, {"seg": s + db}, {"seg": s + dc}
-    at_a, at_b = 1 + c, 2 - c
+    to_diag = {"seg": s + da + db}
 
     def columns(stretch):
         first = stretch * per_dev // GROUP
@@ -52,9 +52,12 @@
         pltpu.make_async_copy(q_hbm, q_ref, local_sem.at[0]),
         pltpu.make_async_copy(branch_hbm.at[:, :, columns(z)], branch.at[OWN, 0], local_sem.at[1]),
         pltpu.make_async_copy(prompt_hbm.at[:, :, columns(z)], own_prompt, local_sem.at[2]),
+        pltpu.make_async_copy(anc_hbm, anc_ref, local_sem.at[3]),
+        pltpu.make_async_copy(seg_hbm, seg_ref, local_sem.at[4]),
+        pltpu.make_async_copy(cnt_hbm, cnt_ref, local_sem.at[5]),
     ]
     barrier = pltpu.get_barrier_semaphore()
-    partners = [to_a, to_b, to_sib]
+    partners = [to_a, to_b, to_sib, to_diag]
     partners += [{"stretch": (z + j) % stretch_count} for j in range(1, stretch_count)]
     partners += [{"seg": (g + j) % groups * CUBE + r} for j in range(1, groups)]
     for partner in partners:
@@ -76,11 +79,12 @@
     def arrived(target, recv_sem):
         pltpu.make_async_copy(target, target, recv_sem).wait()
 
-    quarter = pl.ds(pl.multiple_of(chip * part, 16), part)
-    for j in range(1, stretch_count):
+    order = list(range(1, stretch_count))
+    order.sort(key=lambda j: abs(2 * j - stretch_count))
+    for j in order:
         other = (z + stretch_count - j) % stretch_count
         send(
-            prompt_hbm.at[c, quarter, columns(other)], prompt.at[c, 0, j - 1],
+            prompt_hbm.at[c, :, columns(other)], prompt.at[c, j - 1],
             z_send.at[j - 1], z_recv.at[j - 1], {"stretch": other},
         )
     for j in range(1, groups):
@@ -112,12 +116,20 @@
         send_branch(OWN, kind, SIB, to_sib)
     for kind in range(2):
         send_branch(OWN, kind, B, to_b)
-
-    def send_prompt(place, target_place, message, device):
-        send(prompt.at[c, place], prompt.at[c, target_place], p_send.at[message], p_recv.at[message], device)
-
-    def prompt_arrived(kind, place, message):
-        arrived(prompt.at[kind, place], p_recv.at[message])
+    for kind in range(2):
+        send_branch(OWN, kind, DIAG, to_diag)
+
+    def pass_prompt(j):
+        arrived(prompt.at[c, j - 1], z_recv.at[j - 1])
+        send(prompt.at[c, j - 1], prompt.at[c, j - 1], p_send.at[j - 1], p_recv.at[j - 1], to_sib)
+
+    def pass_branch(slot, target):
+        for kind in range(2):
+            branch_arrived(slot, kind)
+            send_branch(slot, kind, target, to_sib)
+
+    def prompt_passed(j):
+        arrived(prompt.at[1 - c, j - 1], p_recv.at[j - 1])
 
     def linked_rows(rank, j):
         slot = (g + j) % groups * CUBE + rank
@@ -146,14 +158,14 @@
                 )
         return jnp.concatenate(keys, 0), jnp.concatenate(values, 0)
 
-    def prompt_operands(h):
+    def prompt_operands(pieces, h):
         cols = slice(h * HEAD_DIM, (h + 1) * HEAD_DIM)
-        count = (CUBE // 2) * (stretch_count - 1) * part
-        out = []
-        for kind in range(2):
-            out.append(jnp.concatenate([own_prompt[kind, :, cols], prompt[kind, :, :, :, cols].reshape(count, HEAD_DIM)], 0))
-        keys, values = out
+        blocks = [own_prompt.at[:] if j == 0 else prompt.at[:, j - 1] for j in pieces]
+        keys, values = [jnp.concatenate([block[kind, :, cols] for block in blocks], 0) for kind in range(2)]
         return keys, jnp.concatenate([values, jnp.ones_like(values)], 1)
+
+    def joined(*pairs):
+        return [jnp.concatenate(side, 0) for side in zip(*pairs)]
 
     def attend(h, keys, values, first=False, last=False):
         count = keys.shape[0]
@@ -164,20 +176,22 @@
                 [q_ref[:, (h * sub + i) * HEAD_DIM:(h * sub + i + 1) * HEAD_DIM] for i in range(start, start + heads)], 0
             )
             scores = lax.dot_general(query, keys, (((1,), (1,)), ((), ())), preferred_element_type=jnp.float32)
-            tiles = [scores[:, t:t + HEAD_DIM] for t in range(0, count, HEAD_DIM)]
+            tiles = [scores[:, t:min(t + HEAD_DIM, count)] for t in range(0, count, HEAD_DIM)]
             if first:
                 causal = lax.broadcasted_iota(jnp.int32, (block_rows, HEAD_DIM), 1) <= (
                     lax.broadcasted_iota(jnp.int32, (block_rows, HEAD_DIM), 0) % rows
                 )
                 tiles[0] = jnp.where(causal, tiles[0], HIDDEN)
-            top = functools.reduce(jnp.maximum, tiles)
-            peak = jnp.max(top, -1, keepdims=True)
+            full = [tile for tile in tiles if tile.shape[1] == HEAD_DIM]
+            peak = jnp.max(functools.reduce(jnp.maximum, full), -1, keepdims=True)
+            for tile in tiles[len(full):]:
+                peak = jnp.maximum(peak, jnp.max(tile, -1, keepdims=True))
             if first:
                 peak = jnp.broadcast_to(peak, (block_rows, HEAD_DIM))
             else:
                 former = peak_ref[h, span]
                 peak = jnp.maximum(former, peak)
-            weights = jnp.concatenate([jnp.exp2((tile - peak) * EXP2_SCALE).astype(jnp.bfloat16) for tile in tiles], 1)
+            weights = jnp.concatenate([jnp.exp2((tile - peak[:, :tile.shape[1]]) * EXP2_SCALE).astype(jnp.bfloat16) for tile in tiles], 1)
             both = lax.dot_general(weights, values, (((1,), (0,)), ((), ())), preferred_element_type=jnp.float32)
             acc, tot = both[:, :HEAD_DIM], both[:, HEAD_DIM:]
             if not first:
@@ -197,52 +211,31 @@
     loads[0].wait()
     if groups == 1:
         loads[1].wait()
-    loads[2].wait()
+    for load in loads[2:]:
+        load.wait()
     for kind in range(2):
         branch_arrived(SIB, kind)
     for h in range(kv_per):
-        attend(h, *operands([OWN, SIB] if groups == 1 else [OWN], h), first=True)
-    for j in range(1, stretch_count):
-        arrived(prompt.at[c, 0, j - 1], z_recv.at[j - 1])
-    send_prompt(0, at_a, 0, to_a)
-    send_prompt(0, at_b, 1, to_b)
-    send_prompt(0, 0, 3, to_sib)
-    for kind in range(2):
-        branch_arrived(A, kind)
-        send_branch(A, kind, DIAG, to_b)
-        send_branch(A, kind, SIB_A, to_sib)
-    for kind in range(2):
-        branch_arrived(B, kind)
-        send_branch(B, kind, SIB_B, to_sib)
+        attend(h, *joined(operands([OWN, SIB], h), prompt_operands([0], h)), first=True)
+    pass_branch(A, SIB_A)
+    pass_branch(B, SIB_B)
     for slot in (SIB_A, SIB_B):
         for kind in range(2):
             branch_arrived(slot, kind)
-    near = [A, B, SIB_A, SIB_B]
-    if groups > 1:
-        near = [SIB] + near
-    attend(0, *operands(near, 0))
-    prompt_arrived(c, at_a, 0)
-    send_prompt(at_a, 3, 2, to_b)
-    send_prompt(at_a, at_a, 4, to_sib)
-    prompt_arrived(c, at_b, 1)
-    send_prompt(at_b, at_b, 5, to_sib)
-    for kind in range(2):
-        branch_arrived(DIAG, kind)
-        send_branch(DIAG, kind, SIB_DIAG, to_sib)
-    for h in range(1, kv_per):
-        attend(h, *operands(near, h))
-    prompt_arrived(c, 3, 2)
-    send_prompt(3, 3, 6, to_sib)
+    for h in range(kv_per):
+        attend(h, *operands([A, B, SIB_A, SIB_B], h))
+        if h == 0:
+            pass_branch(DIAG, SIB_DIAG)
     for kind in range(2):
         branch_arrived(SIB_DIAG, kind)
     for h in range(kv_per):
         attend(h, *operands([DIAG, SIB_DIAG], h))
-    prompt_arrived(1 - c, 0, 3)
-    prompt_arrived(1 - c, at_b, 4)
-    prompt_arrived(1 - c, at_a, 5)
-    prompt_arrived(1 - c, 3, 6)
-    for h in range(kv_per):
-        attend(h, *prompt_operands(h), last=True)
+    for j in reversed(order):
+        pass_prompt(j)
+    for j in order:
+        prompt_passed(j)
+    for h in range(kv_per):
+        attend(h, *prompt_operands(order, h), last=True)
     for copy in sent:
         copy.wait_send()
 
@@ -256,30 +249,31 @@
     sub = per_dev // kv_per
     width = kv_per * HEAD_DIM
     groups = seg_count // CUBE
-    part = prompt_kv.shape[1] // (CUBE // 2)
     state = pltpu.VMEM((kv_per, sub * rows, HEAD_DIM), jnp.float32)
     dma = pltpu.SemaphoreType.DMA
-    smem = pl.BlockSpec(memory_space=pltpu.SMEM)
     hbm = pl.BlockSpec(memory_space=pl.ANY)
     return pl.pallas_call(
-        functools.partial(kernel, seg_count, stretch_count, min(sub, 4) * rows),
+        functools.partial(kernel, seg_count, stretch_count, min(sub, 8) * rows),
         out_shape=jax.ShapeDtypeStruct((rows, features), jnp.bfloat16),
-        in_specs=[smem, smem, smem, hbm, hbm, hbm],
+        in_specs=[hbm] * 6,
         out_specs=pl.BlockSpec(memory_space=pltpu.VMEM),
         scratch_shapes=[
+            pltpu.SMEM(ancestry.shape, jnp.int32),
+            pltpu.SMEM(segment_of_slot.shape, jnp.int32),
+            pltpu.SMEM(counts.shape, jnp.int32),
             pltpu.VMEM((rows, features), jnp.bfloat16),
             pltpu.VMEM((2, prompt_kv.shape[1], width), jnp.bfloat16),
             pltpu.VMEM((CUBE, groups, 2, rows, width), jnp.bfloat16),
-            pltpu.VMEM((2, CUBE // 2, stretch_count - 1, part, width), jnp.bfloat16),
+            pltpu.VMEM((2, stretch_count - 1, prompt_kv.shape[1], width), jnp.bfloat16),
             state, state, state,
-            dma((3,)),
+            dma((6,)),
             dma((stretch_count - 1,)), dma((stretch_count - 1,)),
             dma((max(1, groups - 1),)), dma((max(1, groups - 1),)),
             dma((8, 2)), dma((8, 2)),
-            dma((7,)), dma((7,)),
+            dma((stretch_count - 1,)), dma((stretch_count - 1,)),
         ],
         compiler_params=pltpu.CompilerParams(
-            collective_id=0, has_side_effects=True, vmem_limit_bytes=40 * 1024 * 1024
+            collective_id=0, has_side_effects=True, vmem_limit_bytes=62 * 1024 * 1024
         ),
     )(ancestry, segment_of_slot, counts, queries, branch_kv, prompt_kv)
 

time: 27.6 us -> 22.8 us (0.83)
  local copies, waits for them, and re-layouts: 6.01 us -> 1.88 us
  Pallas kernels: 21.3 us -> 20.8 us
    unnamed x13 -> x1, local copies, waits for them, and re-layouts: 6.01 us -> 1.88 us
    pallas_call x1, Pallas kernels: 21.3 us -> 20.8 us  [local(): pl.pallas_call(functools.partial(kernel, seg_count, stretch_count, min(su...]
where the time goes in v2:
time: 22.8 us; the launch traced here: 22.7 us
  Pallas kernels  20.8 us (91%)
  local copies, waits for them, and re-layouts  1.88 us (8%)
    pallas_call x1, Pallas kernels, local(): pl.pallas_call(functools.partial(kernel, seg_count, stretch_count, min(su...  20.8 us
    unnamed x1, local copies, waits for them, and re-layouts  1.88 us

profile of v2, /device:TPU:0, one launch (start us, length us, event | category | flops | bytes accessed | tf_op | source)
XLA Modules:
  0.0 22.7 jit_solution(8561659245267195040)
XLA Ops:
  0.0 20.8 %shard_map.64 = bf16[128,2048]{1,0:T(8,128)(2,1)} custom-call(s32[8,8]{1,0:T(8,128)} %anc_hbm.1, s32[8]{0:T(128)} %seg_hbm.1, s32[8]{0:T(128)} %cnt_hbm.1, bf16[128,2048]{1,0:T(8,128)(2,1)} %q_hbm.1, bf16[2,128,1024]{2,1,0:T(8,128)(2,1)} %branch_hbm.1, bf16[2,192,1024]{2,1,0:T(8,128)(2,1)} %prompt_hbm.1), custom_call_target="tpu_custom_call" | custom-call | tf_op jit(solution)/shard_map/pallas_call | solution.py:255
  20.8 1.9 %copy.8 = bf16[128,2048]{1,0:T(8,128)(2,1)} copy(bf16[128,2048]{1,0:T(8,128)(2,1)} %shard_map.64) | data formatting | bytes 1048576

commit v3 on v2

--- a/solution.py
+++ b/solution.py
@@ -80,7 +80,7 @@
         pltpu.make_async_copy(target, target, recv_sem).wait()
 
     order = list(range(1, stretch_count))
-    order.sort(key=lambda j: abs(2 * j - stretch_count))
+    order.sort(key=lambda j: -abs(2 * j - stretch_count))
     for j in order:
         other = (z + stretch_count - j) % stretch_count
         send(
@@ -230,7 +230,7 @@
         branch_arrived(SIB_DIAG, kind)
     for h in range(kv_per):
         attend(h, *operands([DIAG, SIB_DIAG], h))
-    for j in reversed(order):
+    for j in order:
         pass_prompt(j)
     for j in order:
         prompt_passed(j)

time: 22.8 us -> 22.8 us (level)
  no operation moved by 1% of the time
where the time goes in v3:
time: 22.8 us; the launch traced here: 22.7 us
  Pallas kernels  20.8 us (91%)
  local copies, waits for them, and re-layouts  1.88 us (8%)
    pallas_call x1, Pallas kernels, local(): pl.pallas_call(functools.partial(kernel, seg_count, stretch_count, min(su...  20.8 us
    unnamed x1, local copies, waits for them, and re-layouts  1.88 us

profile of v3, /device:TPU:0, one launch (start us, length us, event | category | flops | bytes accessed | tf_op | source)
XLA Modules:
  0.0 22.7 jit_solution(18197366319074265783)
XLA Ops:
  0.0 20.8 %shard_map.64 = bf16[128,2048]{1,0:T(8,128)(2,1)} custom-call(s32[8,8]{1,0:T(8,128)} %anc_hbm.1, s32[8]{0:T(128)} %seg_hbm.1, s32[8]{0:T(128)} %cnt_hbm.1, bf16[128,2048]{1,0:T(8,128)(2,1)} %q_hbm.1, bf16[2,128,1024]{2,1,0:T(8,128)(2,1)} %branch_hbm.1, bf16[2,192,1024]{2,1,0:T(8,128)(2,1)} %prompt_hbm.1), custom_call_target="tpu_custom_call" | custom-call | tf_op jit(solution)/shard_map/pallas_call | solution.py:255
  20.8 1.9 %copy.8 = bf16[128,2048]{1,0:T(8,128)(2,1)} copy(bf16[128,2048]{1,0:T(8,128)(2,1)} %shard_map.64) | data formatting | bytes 1048576
